TPU v7x, 32 devices: a whole 2x2x4 slice. The times are simulated.
32 devices in a mesh: lat: 8 (over y, x, core), lon: 4 (over z).
Axes of the slice: x: 2, y: 2, z: 4, core: 2. Of those that a mesh axis runs over, the one named last changes fastest.
Arguments:
- queries: bfloat16 [128, 64, 1024], P('lat', 'lon'), may hold values from -80 to 80
- keys: bfloat16 [128, 64, 1024], P('lat', 'lon'), may hold values from -6 to 6
- values: bfloat16 [128, 64, 1024], P('lat', 'lon'), may hold values from -6 to 6
- grad_out: bfloat16 [128, 64, 1024], P('lat', 'lon'), may hold values from -6 to 6
- fold_cols: int32 [2, 64], replicated, may hold values from 0 to 63, as said below
Outputs:
- grad_queries: bfloat16 [128, 64, 1024], P('lat', 'lon')
- grad_keys: bfloat16 [128, 64, 1024], P('lat', 'lon')
- grad_values: bfloat16 [128, 64, 1024], P('lat', 'lon')
Inputs may be any that keep to these rules, and one draw needn't show every extreme that they name: Each row of fold_cols maps, for every block b of 16 columns, the runs [b * 16, b * 16 + 4), [b * 16 + 4, (b + 1) * 16 - 4) and [(b + 1) * 16 - 4, (b + 1) * 16) one to one onto the same runs of the block 2 blocks further on the loop.
All inputs are finite; a program needn't handle non-finite values.
Results may differ from a plain program's by a relative error of at most 0.0075.
Values may be sent and summed in bfloat16 or wider, within the bound.
A program may use at most 128 MiB of HBM per device.

v0:
```python
import functools
import math

import jax
import jax.numpy as jnp
from jax import lax
from jax.experimental import pallas as pl
from jax.experimental.pallas import tpu as pltpu
from jax.sharding import PartitionSpec as P

HEAD_DIM = 64
RADIUS = 4
TILE = 16
LANES = 2 * HEAD_DIM
PER_CHUNK = 2

GROUP = 96
CENTER, WEST, EAST = (0, 64), (64, 16), (80, 16)
SLOT = {0: CENTER, -1: WEST, 1: EAST}
BF16 = jnp.bfloat16
F32 = jnp.float32
MESH = pl.DeviceIdType.MESH


def iota(shape, dim):
    return lax.broadcasted_iota(jnp.int32, shape, dim)


def cell_row(cell):
    return jnp.where(cell < 64, cell // 16, (cell - 64) % 16 // 4)


def cell_col(cell):
    side = jnp.where(cell < 80, (cell - 64) % 4, 20 + (cell - 80) % 4)
    return jnp.where(cell < 64, 4 + cell % 16, side)


def dot(a, b, dims):
    return lax.dot_general(a, b, (dims, ((), ())), preferred_element_type=F32)


def kernel(
    lat_count, lon_count, pairs,
    fold, queries, keys, values, grad_out,
    grad_queries, grad_keys, grad_values,
    ext, edge, back, landed, query, gout, total, bias, select, place, turn,
    load_sem, send_sem, recv_sem, back_send_sem, back_recv_sem,
):
    lat = lax.axis_index("lat")
    lon = lax.axis_index("lon")
    half = lon_count // 2
    chunks = pairs // PER_CHUNK
    at_north = lat == 0
    at_south = lat == lat_count - 1

    def loads(pair, which):
        lanes = pl.ds(pl.multiple_of(pair * LANES, LANES), LANES)
        ends = (
            (keys, ext.at[pair, 0, 1:5, 0:64, :]),
            (values, ext.at[pair, 1, 1:5, 0:64, :]),
            (queries, query.at[pair]),
            (grad_out, gout.at[pair]),
        )
        return [
            pltpu.make_async_copy(source.at[:, :, lanes], target, load_sem.at[pair, n])
            for n, (source, target) in enumerate(ends)
            if n // 2 == which
        ]

    for pair in range(pairs):
        for copy in loads(pair, 0):
            copy.start()
    for pair in range(pairs):
        for copy in loads(pair, 1):
            copy.start()

    north = (1, jnp.where(at_north, 0, lat - 1), jnp.where(at_north, half, 0), jnp.where(at_north, 0, 5))
    south = (4, jnp.where(at_south, lat, lat + 1), jnp.where(at_south, half, 0), jnp.where(at_south, 5, 0))
    vertical = []
    for taken, row, shift, lands in (north, south):
        for step in (0, -1, 1):
            device = (row, lax.rem(lon + step + shift + lon_count, lon_count))
            vertical.append((taken, step, device, lands))
    sideways = [(step, (lat, lax.rem(lon + step + lon_count, lon_count))) for step in (-1, 1)]

    barrier = pltpu.get_barrier_semaphore()
    for _, _, device, _ in vertical:
        pl.semaphore_signal(barrier, inc=1, device_id=device, device_id_type=MESH)
    for _, device in sideways:
        pl.semaphore_signal(barrier, inc=1, device_id=device, device_id_type=MESH)

    def span(chunk):
        return pl.ds(chunk * PER_CHUNK, PER_CHUNK)

    def part(buffer, chunk, group, step):
        start, size = SLOT[step]
        return buffer.at[span(chunk), :, group, pl.ds(start, size), :]

    def side(buffer, chunk, step):
        start, size = SLOT[step]
        return buffer.at[span(chunk), :, 1:5, pl.ds(start, size), :]

    def slot_index(group_is_south, step):
        return 3 * group_is_south + {0: 0, -1: 1, 1: 2}[step]

    def sends(chunk, outgoing, incoming, send, recv, first):
        copies = []
        for n, (step, device) in enumerate(sideways):
            source = edge.at[span(chunk), :, n] if first else side(outgoing, chunk, step)
            copies.append(pltpu.make_async_remote_copy(
                src_ref=source, dst_ref=side(incoming, chunk, -step),
                send_sem=send.at[chunk, 6 + n], recv_sem=recv.at[chunk, 7 - n],
                device_id=device, device_id_type=MESH,
            ))
        for n, (taken, step, device, lands) in enumerate(vertical):
            if not first:
                source = part(outgoing, chunk, 0 if taken == 1 else 5, step)
            elif step == 0:
                source = part(outgoing, chunk, taken, 0)
            else:
                source = edge.at[span(chunk), :, 0 if step < 0 else 1, taken - 1]
            copies.append(pltpu.make_async_remote_copy(
                src_ref=source, dst_ref=part(incoming, chunk, lands, -step),
                send_sem=send.at[chunk, n],
                recv_sem=recv.at[chunk, slot_index(lands // 5, -step)],
                device_id=device, device_id_type=MESH,
            ))
        return copies

    def arrivals(chunk, incoming, send, recv):
        copies = []
        for n, (step, device) in enumerate(sideways):
            ref = side(incoming, chunk, step)
            copies.append(pltpu.make_async_remote_copy(
                src_ref=ref, dst_ref=ref, send_sem=send.at[chunk, 6 + n],
                recv_sem=recv.at[chunk, 6 + n], device_id=device, device_id_type=MESH,
            ))
        for group in (0, 5):
            for step in (0, -1, 1):
                ref = part(incoming, chunk, group, step)
                n = slot_index(group // 5, step)
                copies.append(pltpu.make_async_remote_copy(
                    src_ref=ref, dst_ref=ref, send_sem=send.at[chunk, n],
                    recv_sem=recv.at[chunk, n],
                    device_id=sideways[0][1], device_id_type=MESH,
                ))
        return copies

    row = iota((128, 256), 0)
    col = iota((128, 256), 1)
    wanted = (row % 64 // 4) * 16 + row % 4 + jnp.where(row < 64, 0, 12)
    select[...] = (col == wanted).astype(F32).astype(BF16)

    pl.semaphore_wait(barrier, 8)

    def pack(chunk, carry):
        for inner in range(PER_CHUNK):
            pair = chunk * PER_CHUNK + inner
            for copy in loads(pair, 0):
                copy.wait()
            for kind in range(2):
                cells = ext[pair, kind, 1:5, 0:64, :].reshape(256, LANES)
                packed = dot(select[...], cells, ((1,), (0,))).astype(BF16)
                edge[pair, kind] = packed.reshape(2, 4, 16, LANES)
        for copy in sends(chunk, ext, ext, send_sem, recv_sem, True):
            copy.start()
        return carry

    lax.fori_loop(0, chunks, pack, 0)

    key = iota((4 * GROUP, 128), 0)
    asker = iota((4 * GROUP, 128), 1)
    row_gap = key // GROUP * 4 + cell_row(key % GROUP) - RADIUS - asker // 16
    col_gap = cell_col(key % GROUP) - RADIUS - asker % 16
    seen = (jnp.abs(row_gap) <= RADIUS) & (jnp.abs(col_gap) <= RADIUS)
    bias[...] = jnp.where(seen, 0.0, -1e30)

    row = iota((256, 192), 0)
    col = iota((256, 192), 1)
    target = jnp.clip(col // 32 - 1, 0, 3) * 64 + (col % 16 // 4) * 16 + col % 4
    target = target + jnp.where(col % 32 < 16, 0, 12)
    place[...] = (row == target).astype(F32).astype(BF16)

    @pl.when(at_north | at_south)
    def _():
        row = iota((GROUP, GROUP), 0)
        col = iota((GROUP, GROUP), 1)
        padded_col = cell_col(row)
        source_col = jnp.zeros((GROUP, GROUP), jnp.int32)
        pole = jnp.where(at_north, 0, 1)
        for place_col in range(TILE + 2 * RADIUS):
            grid_col = lax.rem(
                lon * TILE + (place_col - RADIUS) + lon_count * TILE, lon_count * TILE
            )
            within = fold[pole, grid_col] % TILE
            within = within + (-8 if place_col < 4 else 4 if place_col < 20 else 20) - (
                4 if place_col < 4 else 0
            )
            source_col = jnp.where(padded_col == place_col, within, source_col)
        hit = (cell_col(col) == source_col) & (cell_row(col) == 3 - cell_row(row))
        turn[...] = hit.astype(F32).astype(BF16)

    pole_group = jnp.where(at_north, 0, 5)
    low = iota((128, LANES), 1) < HEAD_DIM
    rate = HEAD_DIM ** -0.5
    exponent = rate * math.log2(math.e)

    def by_head(cells):
        zero = jnp.zeros_like(cells)
        return jnp.concatenate([jnp.where(low, cells, zero), jnp.where(low, zero, cells)], axis=0)

    def attend(pair, tile):
        seen_keys = ext[pair, 0, 2 * tile : 2 * tile + 4].reshape(4 * GROUP, LANES)
        seen_values = ext[pair, 1, 2 * tile : 2 * tile + 4].reshape(4 * GROUP, LANES)
        asking = by_head(query[pair, 2 * tile : 2 * tile + 2].reshape(128, LANES))
        grads = by_head(gout[pair, 2 * tile : 2 * tile + 2].reshape(128, LANES))
        outside = jnp.concatenate([bias[...], bias[...]], axis=1)
        scores = dot(seen_keys, asking, ((1,), (1,))) + outside
        top = jnp.max(scores, axis=0, keepdims=True)
        raised = jnp.exp2((scores - top) * exponent)
        weights = raised * (1.0 / jnp.sum(raised, axis=0, keepdims=True))
        dweights = dot(seen_values, grads, ((1,), (1,)))
        correction = jnp.sum(weights * dweights, axis=0, keepdims=True)
        dscores = (weights * (dweights - correction)).astype(BF16)
        dkey = dot(dscores, asking, ((1,), (0,))) * rate
        dvalue = dot(weights.astype(BF16), grads, ((1,), (0,)))
        dquery = dot(dscores, seen_keys, ((0,), (0,)))
        dquery = jnp.where(low, dquery[:128], dquery[128:]) * rate
        lanes = pl.ds(pl.multiple_of(pair * LANES, LANES), LANES)
        grad_queries[128 * tile : 128 * tile + 128, lanes] = dquery.astype(BF16)
        return dkey, dvalue

    def turn_pole(buffer, chunk, dims):
        @pl.when(at_north | at_south)
        def _():
            for inner in range(PER_CHUNK):
                pair = chunk * PER_CHUNK + inner
                both = jnp.concatenate(
                    [buffer[pair, 0, pole_group], buffer[pair, 1, pole_group]], axis=1
                )
                turned = dot(turn[...], both, dims).astype(BF16)
                buffer[pair, 0, pole_group] = turned[:, :LANES]
                buffer[pair, 1, pole_group] = turned[:, LANES:]

    def work(chunk, carry):
        for inner in range(PER_CHUNK):
            for copy in loads(chunk * PER_CHUNK + inner, 1):
                copy.wait()
        for copy in arrivals(chunk, ext, send_sem, recv_sem):
            copy.wait_recv()
        turn_pole(ext, chunk, ((1,), (0,)))
        for inner in range(PER_CHUNK):
            pair = chunk * PER_CHUNK + inner
            upper = attend(pair, 0)
            lower = attend(pair, 1)
            for kind in range(2):
                whole = jnp.concatenate(
                    [
                        upper[kind][: 2 * GROUP],
                        upper[kind][2 * GROUP :] + lower[kind][: 2 * GROUP],
                        lower[kind][2 * GROUP :],
                    ],
                    axis=0,
                ).reshape(6, GROUP, LANES)
                back[pair, kind] = whole.astype(BF16)
                total[pair, kind] = whole[1:5, 0:64].reshape(256, LANES)
        turn_pole(back, chunk, ((0,), (0,)))
        for copy in sends(chunk, back, landed, back_send_sem, back_recv_sem, False):
            copy.start()
        return carry

    lax.fori_loop(0, chunks, work, 0)

    def finish(chunk, carry):
        for copy in arrivals(chunk, landed, back_send_sem, back_recv_sem):
            copy.wait_recv()
        for inner in range(PER_CHUNK):
            pair = chunk * PER_CHUNK + inner
            lanes = pl.ds(pl.multiple_of(pair * LANES, LANES), LANES)
            for kind, out in ((0, grad_keys), (1, grad_values)):
                sides = landed[pair, kind, :, 64:96, :].reshape(192, LANES)
                whole = total[pair, kind] + dot(place[...], sides, ((1,), (0,)))
                first = whole[:64] + landed[pair, kind, 0, 0:64, :].astype(F32)
                last = whole[192:] + landed[pair, kind, 5, 0:64, :].astype(F32)
                out[0:64, lanes] = first.astype(BF16)
                out[64:192, lanes] = whole[64:192].astype(BF16)
                out[192:256, lanes] = last.astype(BF16)
        return carry

    lax.fori_loop(0, chunks, finish, 0)

    def drain(chunk, carry):
        for copy in sends(chunk, ext, ext, send_sem, recv_sem, True):
            copy.wait_send()
        for copy in sends(chunk, back, landed, back_send_sem, back_recv_sem, False):
            copy.wait_send()
        return carry

    lax.fori_loop(0, chunks, drain, 0)


def on_device(lat_count, lon_count, queries, keys, values, grad_out, fold_cols):
    height, breadth, features = queries.shape
    pairs = features // LANES
    chunks = pairs // PER_CHUNK
    cells = height * breadth
    inputs = [a.reshape(4, 64, features) for a in (queries, keys, values, grad_out)]
    window = (pairs, 2, 6, GROUP, LANES)
    out = jax.ShapeDtypeStruct((cells, features), BF16)
    results = pl.pallas_call(
        functools.partial(kernel, lat_count, lon_count, pairs),
        out_shape=(out, out, out),
        in_specs=[pl.BlockSpec(memory_space=pltpu.SMEM)]
        + [pl.BlockSpec(memory_space=pl.ANY)] * 4,
        out_specs=[pl.BlockSpec(memory_space=pltpu.VMEM)] * 3,
        scratch_shapes=[
            pltpu.VMEM(window, BF16),
            pltpu.VMEM((pairs, 2, 2, 4, 16, LANES), BF16),
            pltpu.VMEM(window, BF16),
            pltpu.VMEM(window, BF16),
            pltpu.VMEM((pairs, 4, 64, LANES), BF16),
            pltpu.VMEM((pairs, 4, 64, LANES), BF16),
            pltpu.VMEM((pairs, 2, cells, LANES), F32),
            pltpu.VMEM((4 * GROUP, 128), F32),
            pltpu.VMEM((128, 256), BF16),
            pltpu.VMEM((256, 192), BF16),
            pltpu.VMEM((GROUP, GROUP), BF16),
            pltpu.SemaphoreType.DMA((pairs, 4)),
        ]
        + [pltpu.SemaphoreType.DMA((chunks, 8))] * 4,
        compiler_params=pltpu.CompilerParams(
            collective_id=0, has_side_effects=True, vmem_limit_bytes=44 << 20
        ),
        cost_estimate=pl.CostEstimate(
            flops=2_000_000_000, bytes_accessed=4_000_000, transcendentals=1_600_000
        ),
    )(fold_cols, *inputs)
    return tuple(r.reshape(height, breadth, features) for r in results)


def solution(mesh):
    block = P("lat", "lon", None)
    return jax.shard_map(
        functools.partial(on_device, mesh.shape["lat"], mesh.shape["lon"]),
        mesh=mesh,
        in_specs=(block, block, block, block, P()),
        out_specs=(block, block, block),
        check_vma=False,
    )
```

profile of v0, /device:TPU:0, one launch (start us, length us, event | category | flops | bytes accessed | tf_op | source)
XLA Modules:
  0.0 63.0 jit_solution(6139853562016575879)
XLA Ops:
  0.6 0.0 copy-start.4
  0.6 0.7 %copy-done.4 = s32[2,64]{1,0:T(2,128)S(1)} copy-done((s32[2,64]{1,0:T(2,128)S(1)}, s32[2,64]{1,0:T(2,128)}, u32[]{:S(2)}) %copy-start.4) | copy-done | bytes 536
  1.3 0.0 copy-start
  1.3 1.0 %copy-done = bf16[16,16,1024]{2,1,0:T(8,128)(2,1)S(1)} copy-done((bf16[16,16,1024]{2,1,0:T(8,128)(2,1)S(1)}, bf16[16,16,1024]{2,1,0:T(8,128)(2,1)}, u32[]{:S(2)}) %copy-start) | copy-done | bytes 524312
  2.4 0.0 copy-start.1
  2.4 1.0 %copy-done.1 = bf16[16,16,1024]{2,1,0:T(8,128)(2,1)S(1)} copy-done((bf16[16,16,1024]{2,1,0:T(8,128)(2,1)S(1)}, bf16[16,16,1024]{2,1,0:T(8,128)(2,1)}, u32[]{:S(2)}) %copy-start.1) | copy-done | bytes 524312
  3.4 0.0 copy-start.2
  3.4 1.0 %copy-done.2 = bf16[16,16,1024]{2,1,0:T(8,128)(2,1)S(1)} copy-done((bf16[16,16,1024]{2,1,0:T(8,128)(2,1)S(1)}, bf16[16,16,1024]{2,1,0:T(8,128)(2,1)}, u32[]{:S(2)}) %copy-start.2) | copy-done | bytes 524312
  4.4 0.0 copy-start.3
  4.4 1.0 %copy-done.3 = bf16[16,16,1024]{2,1,0:T(8,128)(2,1)S(1)} copy-done((bf16[16,16,1024]{2,1,0:T(8,128)(2,1)S(1)}, bf16[16,16,1024]{2,1,0:T(8,128)(2,1)}, u32[]{:S(2)}) %copy-start.3) | copy-done | bytes 524312
  5.5 55.1 %shard_map.76 = (bf16[256,1024]{1,0:T(8,128)(2,1)S(1)}, bf16[256,1024]{1,0:T(8,128)(2,1)S(1)}, bf16[256,1024]{1,0:T(8,128)(2,1)S(1)}) custom-call(s32[2,64]{1,0:T(2,128)S(1)} %copy-done.4, bf16[4,64,1024]{2,1,0:T(8,128)(2,1)S(1)} %bitcast.10, bf16[4,64,1024]{2,1,0:T(8,128)(2,1)S(1)} %bitcast.11, bf16[4,64,1024]{2,1,0:T(8,128)(2,1)S(1)} %bitcast.12, ...), custom_call_target="tpu_custom_call" | custom-call | flops 2000000000 | bytes 4000000 | tf_op jit(solution)/shard_map/pallas_call | solution.py:310
  60.6 0.8 %copy.11 = bf16[16,16,1024]{2,1,0:T(8,128)(2,1)} copy(bf16[16,16,1024]{2,1,0:T(8,128)(2,1)S(1)} %bitcast.9) | data formatting | bytes 1048576
  61.4 0.8 %copy.12 = bf16[16,16,1024]{2,1,0:T(8,128)(2,1)} copy(bf16[16,16,1024]{2,1,0:T(8,128)(2,1)S(1)} %bitcast.8) | data formatting | bytes 1048576
  62.2 0.8 %copy.13 = bf16[16,16,1024]{2,1,0:T(8,128)(2,1)} copy(bf16[16,16,1024]{2,1,0:T(8,128)(2,1)S(1)} %bitcast.7) | data formatting | bytes 1048576
Async XLA Ops:
  0.6 0.7 %copy-start.4 = (s32[2,64]{1,0:T(2,128)S(1)}, s32[2,64]{1,0:T(2,128)}, u32[]{:S(2)}) copy-start(s32[2,64]{1,0:T(2,128)} %fold.1) | copy-start | bytes 1540
  1.3 1.0 %copy-start = (bf16[16,16,1024]{2,1,0:T(8,128)(2,1)S(1)}, bf16[16,16,1024]{2,1,0:T(8,128)(2,1)}, u32[]{:S(2)}) copy-start(bf16[16,16,1024]{2,1,0:T(8,128)(2,1)} %param.5) | copy-start | bytes 1572868
  2.4 1.0 %copy-start.1 = (bf16[16,16,1024]{2,1,0:T(8,128)(2,1)S(1)}, bf16[16,16,1024]{2,1,0:T(8,128)(2,1)}, u32[]{:S(2)}) copy-start(bf16[16,16,1024]{2,1,0:T(8,128)(2,1)} %param.6) | copy-start | bytes 1572868
  3.4 1.0 %copy-start.2 = (bf16[16,16,1024]{2,1,0:T(8,128)(2,1)S(1)}, bf16[16,16,1024]{2,1,0:T(8,128)(2,1)}, u32[]{:S(2)}) copy-start(bf16[16,16,1024]{2,1,0:T(8,128)(2,1)} %param.7) | copy-start | bytes 1572868
  4.4 1.0 %copy-start.3 = (bf16[16,16,1024]{2,1,0:T(8,128)(2,1)S(1)}, bf16[16,16,1024]{2,1,0:T(8,128)(2,1)}, u32[]{:S(2)}) copy-start(bf16[16,16,1024]{2,1,0:T(8,128)(2,1)} %param.8) | copy-start | bytes 1572868
where the time goes:
time: 63.3 us; the launch traced here: 63 us
  Pallas kernels  55.1 us (87%)
  local copies, waits for them, and re-layouts  7.22 us (11%)
  between operations  0.65 us (1%)
    pallas_call x1, Pallas kernels, on_device(): pl.pallas_call(functools.partial(kernel, lat_count, lon_count, pairs), ou...  55.1 us
    unnamed x13, local copies, waits for them, and re-layouts  7.22 us

commit v1 on v0

--- a/solution.py
+++ b/solution.py
@@ -74,20 +74,31 @@
         for copy in loads(pair, 1):
             copy.start()
 
-    north = (1, jnp.where(at_north, 0, lat - 1), jnp.where(at_north, half, 0), jnp.where(at_north, 0, 5))
-    south = (4, jnp.where(at_south, lat, lat + 1), jnp.where(at_south, half, 0), jnp.where(at_south, 5, 0))
-    vertical = []
-    for taken, row, shift, lands in (north, south):
-        for step in (0, -1, 1):
-            device = (row, lax.rem(lon + step + shift + lon_count, lon_count))
-            vertical.append((taken, step, device, lands))
-    sideways = [(step, (lat, lax.rem(lon + step + lon_count, lon_count))) for step in (-1, 1)]
+    directions = (
+        (1, 0, 0, at_north, 5, jnp.where(at_north, 0, lat - 1)),
+        (4, 5, 5, at_south, 0, jnp.where(at_south, lat, lat + 1)),
+    )
+
+    def around(step):
+        return lax.rem(lon + step + lon_count, lon_count)
+
+    sideways = [(step, (lat, around(step))) for step in (-1, 1)]
 
     barrier = pltpu.get_barrier_semaphore()
-    for _, _, device, _ in vertical:
-        pl.semaphore_signal(barrier, inc=1, device_id=device, device_id_type=MESH)
+    for _, _, _, polar, _, row in directions:
+        pl.semaphore_signal(
+            barrier, inc=1, device_id=(row, jnp.where(polar, around(half), lon)),
+            device_id_type=MESH,
+        )
     for _, device in sideways:
         pl.semaphore_signal(barrier, inc=1, device_id=device, device_id_type=MESH)
+
+    @pl.when(at_north | at_south)
+    def _():
+        for step in (-1, 1):
+            pl.semaphore_signal(
+                barrier, inc=1, device_id=(lat, around(step + half)), device_id_type=MESH
+            )
 
     def span(chunk):
         return pl.ds(chunk * PER_CHUNK, PER_CHUNK)
@@ -103,47 +114,85 @@
     def slot_index(group_is_south, step):
         return 3 * group_is_south + {0: 0, -1: 1, 1: 2}[step]
 
-    def sends(chunk, outgoing, incoming, send, recv, first):
-        copies = []
+    def remote(source, target, send, recv, device):
+        return pltpu.make_async_remote_copy(
+            src_ref=source, dst_ref=target, send_sem=send, recv_sem=recv,
+            device_id=device, device_id_type=MESH,
+        )
+
+    def stage(first):
+        if first:
+            return ext, ext, send_sem, recv_sem
+        return back, landed, back_send_sem, back_recv_sem
+
+    def send_sideways(chunk, first):
+        outgoing, incoming, send, recv = stage(first)
         for n, (step, device) in enumerate(sideways):
             source = edge.at[span(chunk), :, n] if first else side(outgoing, chunk, step)
-            copies.append(pltpu.make_async_remote_copy(
-                src_ref=source, dst_ref=side(incoming, chunk, -step),
-                send_sem=send.at[chunk, 6 + n], recv_sem=recv.at[chunk, 7 - n],
-                device_id=device, device_id_type=MESH,
-            ))
-        for n, (taken, step, device, lands) in enumerate(vertical):
-            if not first:
-                source = part(outgoing, chunk, 0 if taken == 1 else 5, step)
-            elif step == 0:
-                source = part(outgoing, chunk, taken, 0)
-            else:
-                source = edge.at[span(chunk), :, 0 if step < 0 else 1, taken - 1]
-            copies.append(pltpu.make_async_remote_copy(
-                src_ref=source, dst_ref=part(incoming, chunk, lands, -step),
-                send_sem=send.at[chunk, n],
-                recv_sem=recv.at[chunk, slot_index(lands // 5, -step)],
-                device_id=device, device_id_type=MESH,
-            ))
-        return copies
-
-    def arrivals(chunk, incoming, send, recv):
+            remote(
+                source, side(incoming, chunk, -step),
+                send.at[chunk, 6 + n], recv.at[chunk, 7 - n], device,
+            ).start()
+
+    def send_rows(chunk, first):
+        outgoing, incoming, send, recv = stage(first)
+        for n, (taken, halo, across, polar, lands, row) in enumerate(directions):
+            group = jnp.where(polar, across, lands)
+            remote(
+                part(outgoing, chunk, taken if first else halo, 0),
+                part(incoming, chunk, group, 0),
+                send.at[chunk, 3 * n], recv.at[chunk, slot_index(group // 5, 0)],
+                (row, jnp.where(polar, around(half), lon)),
+            ).start()
+
+    def send_corners_across(chunk, first):
+        outgoing, incoming, send, recv = stage(first)
+        for n, (taken, halo, across, polar, lands, row) in enumerate(directions):
+            @pl.when(polar)
+            def _():
+                for step in (-1, 1):
+                    if first:
+                        source = edge.at[span(chunk), :, 0 if step < 0 else 1, taken - 1]
+                    else:
+                        source = part(outgoing, chunk, halo, step)
+                    remote(
+                        source, part(incoming, chunk, across, -step),
+                        send.at[chunk, slot_index(n, step)],
+                        recv.at[chunk, slot_index(across // 5, -step)],
+                        (lat, around(step + half)),
+                    ).start()
+
+    def send_corners(chunk, first):
+        outgoing, incoming, send, recv = stage(first)
+        for n, (taken, halo, across, polar, lands, row) in enumerate(directions):
+            @pl.when(jnp.logical_not(polar))
+            def _():
+                for step in (-1, 1):
+                    remote(
+                        part(outgoing, chunk, taken if first else halo, step),
+                        part(incoming, chunk, lands, step),
+                        send.at[chunk, slot_index(n, step)],
+                        recv.at[chunk, slot_index(lands // 5, step)],
+                        (row, lon),
+                    ).start()
+
+    def side_ends(chunk, first):
+        outgoing, incoming, send, recv = stage(first)
         copies = []
         for n, (step, device) in enumerate(sideways):
             ref = side(incoming, chunk, step)
-            copies.append(pltpu.make_async_remote_copy(
-                src_ref=ref, dst_ref=ref, send_sem=send.at[chunk, 6 + n],
-                recv_sem=recv.at[chunk, 6 + n], device_id=device, device_id_type=MESH,
-            ))
-        for group in (0, 5):
-            for step in (0, -1, 1):
-                ref = part(incoming, chunk, group, step)
-                n = slot_index(group // 5, step)
-                copies.append(pltpu.make_async_remote_copy(
-                    src_ref=ref, dst_ref=ref, send_sem=send.at[chunk, n],
-                    recv_sem=recv.at[chunk, n],
-                    device_id=sideways[0][1], device_id_type=MESH,
-                ))
+            copies.append(remote(ref, ref, send.at[chunk, 6 + n], recv.at[chunk, 6 + n], device))
+        return copies
+
+    def part_ends(chunk, first, group, steps):
+        outgoing, incoming, send, recv = stage(first)
+        copies = []
+        for step in steps:
+            ref = part(incoming, chunk, group, step)
+            n = slot_index(group // 5, step)
+            copies.append(
+                remote(ref, ref, send.at[chunk, n], recv.at[chunk, n], sideways[0][1])
+            )
         return copies
 
     row = iota((128, 256), 0)
@@ -151,7 +200,7 @@
     wanted = (row % 64 // 4) * 16 + row % 4 + jnp.where(row < 64, 0, 12)
     select[...] = (col == wanted).astype(F32).astype(BF16)
 
-    pl.semaphore_wait(barrier, 8)
+    pl.semaphore_wait(barrier, jnp.where(at_north | at_south, 6, 4))
 
     def pack(chunk, carry):
         for inner in range(PER_CHUNK):
@@ -162,8 +211,9 @@
                 cells = ext[pair, kind, 1:5, 0:64, :].reshape(256, LANES)
                 packed = dot(select[...], cells, ((1,), (0,))).astype(BF16)
                 edge[pair, kind] = packed.reshape(2, 4, 16, LANES)
-        for copy in sends(chunk, ext, ext, send_sem, recv_sem, True):
-            copy.start()
+        send_sideways(chunk, True)
+        send_corners_across(chunk, True)
+        send_rows(chunk, True)
         return carry
 
     lax.fori_loop(0, chunks, pack, 0)
@@ -179,7 +229,8 @@
     col = iota((256, 192), 1)
     target = jnp.clip(col // 32 - 1, 0, 3) * 64 + (col % 16 // 4) * 16 + col % 4
     target = target + jnp.where(col % 32 < 16, 0, 12)
-    place[...] = (row == target).astype(F32).astype(BF16)
+    direct = ((col >= 32) | at_north) & ((col < 160) | at_south)
+    place[...] = ((row == target) & direct).astype(F32).astype(BF16)
 
     @pl.when(at_north | at_south)
     def _():
@@ -242,12 +293,32 @@
                 buffer[pair, 0, pole_group] = turned[:, :LANES]
                 buffer[pair, 1, pole_group] = turned[:, LANES:]
 
+    def pass_on(chunk):
+        for copy in side_ends(chunk, True):
+            copy.wait_recv()
+        send_corners(chunk, True)
+
+    def pass_back(chunk):
+        for group, inward, polar in ((0, 1, at_north), (5, 4, at_south)):
+            @pl.when(jnp.logical_not(polar))
+            def _():
+                for copy in part_ends(chunk, False, group, (-1, 1)):
+                    copy.wait_recv()
+                pairs_here = span(chunk)
+                own = back[pairs_here, :, inward, 64:96, :].astype(F32)
+                more = landed[pairs_here, :, group, 64:96, :].astype(F32)
+                back[pairs_here, :, inward, 64:96, :] = (own + more).astype(BF16)
+        send_sideways(chunk, False)
+
+    pass_on(0)
+
     def work(chunk, carry):
         for inner in range(PER_CHUNK):
             for copy in loads(chunk * PER_CHUNK + inner, 1):
                 copy.wait()
-        for copy in arrivals(chunk, ext, send_sem, recv_sem):
-            copy.wait_recv()
+        for group in (0, 5):
+            for copy in part_ends(chunk, True, group, (0, -1, 1)):
+                copy.wait_recv()
         turn_pole(ext, chunk, ((1,), (0,)))
         for inner in range(PER_CHUNK):
             pair = chunk * PER_CHUNK + inner
@@ -264,16 +335,35 @@
                 ).reshape(6, GROUP, LANES)
                 back[pair, kind] = whole.astype(BF16)
                 total[pair, kind] = whole[1:5, 0:64].reshape(256, LANES)
+            if inner == 0:
+                @pl.when(chunk + 1 < chunks)
+                def _():
+                    pass_on(chunk + 1)
+
+                @pl.when(chunk > 0)
+                def _():
+                    pass_back(chunk - 1)
+
         turn_pole(back, chunk, ((0,), (0,)))
-        for copy in sends(chunk, back, landed, back_send_sem, back_recv_sem, False):
-            copy.start()
+        send_corners(chunk, False)
+        send_corners_across(chunk, False)
+        send_rows(chunk, False)
         return carry
 
     lax.fori_loop(0, chunks, work, 0)
+    pass_back(chunks - 1)
 
     def finish(chunk, carry):
-        for copy in arrivals(chunk, landed, back_send_sem, back_recv_sem):
+        for copy in side_ends(chunk, False):
             copy.wait_recv()
+        for group, polar in ((0, at_north), (5, at_south)):
+            for copy in part_ends(chunk, False, group, (0,)):
+                copy.wait_recv()
+
+            @pl.when(polar)
+            def _():
+                for copy in part_ends(chunk, False, group, (-1, 1)):
+                    copy.wait_recv()
         for inner in range(PER_CHUNK):
             pair = chunk * PER_CHUNK + inner
             lanes = pl.ds(pl.multiple_of(pair * LANES, LANES), LANES)
@@ -290,10 +380,12 @@
     lax.fori_loop(0, chunks, finish, 0)
 
     def drain(chunk, carry):
-        for copy in sends(chunk, ext, ext, send_sem, recv_sem, True):
-            copy.wait_send()
-        for copy in sends(chunk, back, landed, back_send_sem, back_recv_sem, False):
-            copy.wait_send()
+        for first in (True, False):
+            for copy in side_ends(chunk, first):
+                copy.wait_send()
+            for group in (0, 5):
+                for copy in part_ends(chunk, first, group, (0, -1, 1)):
+                    copy.wait_send()
         return carry
 
     lax.fori_loop(0, chunks, drain, 0)
@@ -329,7 +421,7 @@
         ]
         + [pltpu.SemaphoreType.DMA((chunks, 8))] * 4,
         compiler_params=pltpu.CompilerParams(
-            collective_id=0, has_side_effects=True, vmem_limit_bytes=44 << 20
+            collective_id=0, has_side_effects=True, vmem_limit_bytes=60 << 20
         ),
         cost_estimate=pl.CostEstimate(
             flops=2_000_000_000, bytes_accessed=4_000_000, transcendentals=1_600_000

time: 63.3 us -> 51.3 us (0.81)
  Pallas kernels: 55.1 us -> 46.5 us
  local copies, waits for them, and re-layouts: 7.22 us -> 3.97 us
    pallas_call x1, Pallas kernels: 55.1 us -> 46.5 us  [on_device(): pl.pallas_call(functools.partial(kernel, lat_count, lon_count, pairs), ou...]
    unnamed x13 -> x7, local copies, waits for them, and re-layouts: 7.22 us -> 3.97 us
where the time goes in v1:
time: 51.3 us; the launch traced here: 51.1 us
  Pallas kernels  46.5 us (91%)
  local copies, waits for them, and re-layouts  3.97 us (8%)
  between operations  0.65 us (1%)
    pallas_call x1, Pallas kernels, on_device(): pl.pallas_call(functools.partial(kernel, lat_count, lon_count, pairs), ou...  46.5 us
    unnamed x7, local copies, waits for them, and re-layouts  3.97 us

profile of v1, /device:TPU:0, one launch (start us, length us, event | category | flops | bytes accessed | tf_op | source)
XLA Modules:
  0.0 51.1 jit_solution(6037126760285106019)
XLA Ops:
  0.6 46.5 %shard_map.76 = (bf16[256,1024]{1,0:T(8,128)(2,1)}, bf16[256,1024]{1,0:T(8,128)(2,1)}, bf16[256,1024]{1,0:T(8,128)(2,1)}) custom-call(s32[2,64]{1,0:T(2,128)} %fold.1, bf16[4,64,1024]{2,1,0:T(8,128)(2,1)} %bitcast.10, bf16[4,64,1024]{2,1,0:T(8,128)(2,1)} %bitcast.11, bf16[4,64,1024]{2,1,0:T(8,128)(2,1)} %bitcast.12, bf16[4,64,1024]{2,1,0:T(8,128)(2,1)} %bitcast.13), custom_call_target="tpu_custom_call" | custom-call | flops 2000000000 | bytes 4000000 | tf_op jit(solution)/shard_map/pallas_call | solution.py:402
  47.1 0.0 copy-start.1
  47.1 1.9 %copy.11 = bf16[16,16,1024]{2,1,0:T(8,128)(2,1)} copy(bf16[16,16,1024]{2,1,0:T(8,128)(2,1)} %bitcast.9) | data formatting | bytes 1048576
  49.1 0.0 copy-done.1
  49.1 0.0 copy-start
  49.1 0.8 %copy.12 = bf16[16,16,1024]{2,1,0:T(8,128)(2,1)} copy(bf16[16,16,1024]{2,1,0:T(8,128)(2,1)S(1)} %bitcast.8) | data formatting | bytes 1048576
  49.9 0.4 copy-done
  50.3 0.8 %copy.13 = bf16[16,16,1024]{2,1,0:T(8,128)(2,1)} copy(bf16[16,16,1024]{2,1,0:T(8,128)(2,1)S(1)} %bitcast.7) | data formatting | bytes 1048576
Async XLA Ops:
  47.1 2.0 %copy-start.1 = (bf16[256,1024]{1,0:T(8,128)(2,1)S(1)}, bf16[256,1024]{1,0:T(8,128)(2,1)}, u32[]{:S(2)}) copy-start(bf16[256,1024]{1,0:T(8,128)(2,1)} %get-tuple-element.7) | copy-start | bytes 1572868
  49.1 1.2 %copy-start = (bf16[256,1024]{1,0:T(8,128)(2,1)S(1)}, bf16[256,1024]{1,0:T(8,128)(2,1)}, u32[]{:S(2)}) copy-start(bf16[256,1024]{1,0:T(8,128)(2,1)} %get-tuple-element.8) | copy-start | bytes 1572868

commit v2 on v1

--- a/solution.py
+++ b/solution.py
@@ -13,6 +13,7 @@
 TILE = 16
 LANES = 2 * HEAD_DIM
 PER_CHUNK = 2
+FIRST_ALONG = False
 
 GROUP = 96
 CENTER, WEST, EAST = (0, 64), (64, 16), (80, 16)
@@ -43,8 +44,8 @@
     lat_count, lon_count, pairs,
     fold, queries, keys, values, grad_out,
     grad_queries, grad_keys, grad_values,
-    ext, edge, back, landed, query, gout, total, bias, select, place, turn,
-    load_sem, send_sem, recv_sem, back_send_sem, back_recv_sem,
+    ext, edge, back, landed, query, gout, total, bias, select, place, turn, hop,
+    load_sem, send_sem, recv_sem, back_send_sem, back_recv_sem, hop_send_sem, hop_recv_sem,
 ):
     lat = lax.axis_index("lat")
     lon = lax.axis_index("lon")
@@ -82,6 +83,14 @@
     def around(step):
         return lax.rem(lon + step + lon_count, lon_count)
 
+    relays = lat == 2
+    relays = relays | (lat == lat_count - 3)
+    at_pole = at_north | at_south
+    relay_row = jnp.where(at_north, 2, lat_count - 3)
+    pole_row = jnp.where(lat == 2, 0, lat_count - 1)
+    to_relay = half if FIRST_ALONG else 0
+    from_relay = 0 if FIRST_ALONG else half
+
     sideways = [(step, (lat, around(step))) for step in (-1, 1)]
 
     barrier = pltpu.get_barrier_semaphore()
@@ -99,6 +108,17 @@
             pl.semaphore_signal(
                 barrier, inc=1, device_id=(lat, around(step + half)), device_id_type=MESH
             )
+        for step in (0, half):
+            pl.semaphore_signal(
+                barrier, inc=1, device_id=(relay_row, around(step)), device_id_type=MESH
+            )
+
+    @pl.when(relays)
+    def _():
+        for step in (0, half):
+            pl.semaphore_signal(
+                barrier, inc=1, device_id=(pole_row, around(step)), device_id_type=MESH
+            )
 
     def span(chunk):
         return pl.ds(chunk * PER_CHUNK, PER_CHUNK)
@@ -137,13 +157,63 @@
     def send_rows(chunk, first):
         outgoing, incoming, send, recv = stage(first)
         for n, (taken, halo, across, polar, lands, row) in enumerate(directions):
-            group = jnp.where(polar, across, lands)
+            group = taken if first else halo
+
+            @pl.when(jnp.logical_not(polar))
+            def _():
+                remote(
+                    part(outgoing, chunk, group, 0), part(incoming, chunk, lands, 0),
+                    send.at[chunk, 3 * n], recv.at[chunk, slot_index(lands // 5, 0)], (row, lon),
+                ).start()
+
+            @pl.when(polar)
+            def _():
+                if first:
+                    remote(
+                        rows_of(outgoing, chunk, 1, group), hop.at[span(chunk)],
+                        send.at[chunk, 8], hop_recv_sem.at[chunk],
+                        (relay_row, around(to_relay)),
+                    ).start()
+                else:
+                    remote(
+                        rows_of(outgoing, chunk, 1, group), rows_of(incoming, chunk, 1, across),
+                        send.at[chunk, 8], recv.at[chunk, 8], (row, around(half)),
+                    ).start()
+                remote(
+                    rows_of(outgoing, chunk, 0, group), rows_of(incoming, chunk, 0, across),
+                    send.at[chunk, 3 * n], recv.at[chunk, 3 * n], (row, around(half)),
+                ).start()
+
+    def rows_of(buffer, chunk, kind, group):
+        return buffer.at[span(chunk), kind, group, pl.ds(0, 64), :]
+
+    def relay(chunk):
+        @pl.when(relays)
+        def _():
+            here = hop.at[span(chunk)]
+            copy = remote(
+                here, rows_of(ext, chunk, 1, jnp.where(lat == 2, 0, 5)),
+                hop_send_sem.at[chunk], recv_sem.at[chunk, 8], (pole_row, around(from_relay)),
+            )
             remote(
-                part(outgoing, chunk, taken if first else halo, 0),
-                part(incoming, chunk, group, 0),
-                send.at[chunk, 3 * n], recv.at[chunk, slot_index(group // 5, 0)],
-                (row, jnp.where(polar, around(half), lon)),
-            ).start()
+                here, here, hop_send_sem.at[chunk], hop_recv_sem.at[chunk], (pole_row, lon)
+            ).wait_recv()
+            copy.start()
+
+    def row_ends(chunk, first, wait):
+        outgoing, incoming, send, recv = stage(first)
+        for n, (taken, halo, across, polar, lands, row) in enumerate(directions):
+            @pl.when(jnp.logical_not(polar))
+            def _():
+                wait(part_ends(chunk, first, across, (0,))[0])
+
+            @pl.when(polar)
+            def _():
+                for kind, at in ((0, 3 * n), (1, 8)):
+                    ref = rows_of(incoming, chunk, kind, across)
+                    wait(remote(
+                        ref, ref, send.at[chunk, at], recv.at[chunk, at], sideways[0][1]
+                    ))
 
     def send_corners_across(chunk, first):
         outgoing, incoming, send, recv = stage(first)
@@ -200,7 +270,7 @@
     wanted = (row % 64 // 4) * 16 + row % 4 + jnp.where(row < 64, 0, 12)
     select[...] = (col == wanted).astype(F32).astype(BF16)
 
-    pl.semaphore_wait(barrier, jnp.where(at_north | at_south, 6, 4))
+    pl.semaphore_wait(barrier, jnp.where(at_pole, 8, jnp.where(relays, 6, 4)))
 
     def pack(chunk, carry):
         for inner in range(PER_CHUNK):
@@ -212,8 +282,8 @@
                 packed = dot(select[...], cells, ((1,), (0,))).astype(BF16)
                 edge[pair, kind] = packed.reshape(2, 4, 16, LANES)
         send_sideways(chunk, True)
+        send_rows(chunk, True)
         send_corners_across(chunk, True)
-        send_rows(chunk, True)
         return carry
 
     lax.fori_loop(0, chunks, pack, 0)
@@ -310,14 +380,20 @@
                 back[pairs_here, :, inward, 64:96, :] = (own + more).astype(BF16)
         send_sideways(chunk, False)
 
+    def relay_all(chunk, carry):
+        relay(chunk)
+        return carry
+
+    lax.fori_loop(0, chunks, relay_all, 0)
     pass_on(0)
 
     def work(chunk, carry):
         for inner in range(PER_CHUNK):
             for copy in loads(chunk * PER_CHUNK + inner, 1):
                 copy.wait()
+        row_ends(chunk, True, lambda copy: copy.wait_recv())
         for group in (0, 5):
-            for copy in part_ends(chunk, True, group, (0, -1, 1)):
+            for copy in part_ends(chunk, True, group, (-1, 1)):
                 copy.wait_recv()
         turn_pole(ext, chunk, ((1,), (0,)))
         for inner in range(PER_CHUNK):
@@ -346,8 +422,8 @@
 
         turn_pole(back, chunk, ((0,), (0,)))
         send_corners(chunk, False)
+        send_rows(chunk, False)
         send_corners_across(chunk, False)
-        send_rows(chunk, False)
         return carry
 
     lax.fori_loop(0, chunks, work, 0)
@@ -356,10 +432,8 @@
     def finish(chunk, carry):
         for copy in side_ends(chunk, False):
             copy.wait_recv()
+        row_ends(chunk, False, lambda copy: copy.wait_recv())
         for group, polar in ((0, at_north), (5, at_south)):
-            for copy in part_ends(chunk, False, group, (0,)):
-                copy.wait_recv()
-
             @pl.when(polar)
             def _():
                 for copy in part_ends(chunk, False, group, (-1, 1)):
@@ -383,9 +457,18 @@
         for first in (True, False):
             for copy in side_ends(chunk, first):
                 copy.wait_send()
+            row_ends(chunk, first, lambda copy: copy.wait_send())
             for group in (0, 5):
-                for copy in part_ends(chunk, first, group, (0, -1, 1)):
+                for copy in part_ends(chunk, first, group, (-1, 1)):
                     copy.wait_send()
+
+        @pl.when(relays)
+        def _():
+            here = hop.at[span(chunk)]
+            remote(
+                here, here, hop_send_sem.at[chunk], hop_recv_sem.at[chunk], (pole_row, lon)
+            ).wait_send()
+
         return carry
 
     lax.fori_loop(0, chunks, drain, 0)
@@ -417,9 +500,11 @@
             pltpu.VMEM((128, 256), BF16),
             pltpu.VMEM((256, 192), BF16),
             pltpu.VMEM((GROUP, GROUP), BF16),
+            pltpu.VMEM((pairs, 64, LANES), BF16),
             pltpu.SemaphoreType.DMA((pairs, 4)),
         ]
-        + [pltpu.SemaphoreType.DMA((chunks, 8))] * 4,
+        + [pltpu.SemaphoreType.DMA((chunks, 9))] * 4
+        + [pltpu.SemaphoreType.DMA((chunks,))] * 2,
         compiler_params=pltpu.CompilerParams(
             collective_id=0, has_side_effects=True, vmem_limit_bytes=60 << 20
         ),

time: 51.3 us -> 51.2 us (level)
  no operation moved by 1% of the time
where the time goes in v2:
time: 51.2 us; the launch traced here: 51 us
  Pallas kernels  46.4 us (91%)
  local copies, waits for them, and re-layouts  3.97 us (8%)
  between operations  0.65 us (1%)
    pallas_call x1, Pallas kernels, on_device(): pl.pallas_call(functools.partial(kernel, lat_count, lon_count, pairs), ou...  46.4 us
    unnamed x7, local copies, waits for them, and re-layouts  3.97 us

profile of v2, /device:TPU:0, one launch (start us, length us, event | category | flops | bytes accessed | tf_op | source)
XLA Modules:
  0.0 51.0 jit_solution(14897592260812930854)
XLA Ops:
  0.6 46.4 %shard_map.76 = (bf16[256,1024]{1,0:T(8,128)(2,1)}, bf16[256,1024]{1,0:T(8,128)(2,1)}, bf16[256,1024]{1,0:T(8,128)(2,1)}) custom-call(s32[2,64]{1,0:T(2,128)} %fold.1, bf16[4,64,1024]{2,1,0:T(8,128)(2,1)} %bitcast.10, bf16[4,64,1024]{2,1,0:T(8,128)(2,1)} %bitcast.11, bf16[4,64,1024]{2,1,0:T(8,128)(2,1)} %bitcast.12, bf16[4,64,1024]{2,1,0:T(8,128)(2,1)} %bitcast.13), custom_call_target="tpu_custom_call" | custom-call | flops 2000000000 | bytes 4000000 | tf_op jit(solution)/shard_map/pallas_call | solution.py:485
  47.0 0.0 copy-start.1
  47.0 1.9 %copy.11 = bf16[16,16,1024]{2,1,0:T(8,128)(2,1)} copy(bf16[16,16,1024]{2,1,0:T(8,128)(2,1)} %bitcast.9) | data formatting | bytes 1048576
  49.0 0.0 copy-done.1
  49.0 0.0 copy-start
  49.0 0.8 %copy.12 = bf16[16,16,1024]{2,1,0:T(8,128)(2,1)} copy(bf16[16,16,1024]{2,1,0:T(8,128)(2,1)S(1)} %bitcast.8) | data formatting | bytes 1048576
  49.8 0.4 copy-done
  50.2 0.8 %copy.13 = bf16[16,16,1024]{2,1,0:T(8,128)(2,1)} copy(bf16[16,16,1024]{2,1,0:T(8,128)(2,1)S(1)} %bitcast.7) | data formatting | bytes 1048576
Async XLA Ops:
  47.0 2.0 %copy-start.1 = (bf16[256,1024]{1,0:T(8,128)(2,1)S(1)}, bf16[256,1024]{1,0:T(8,128)(2,1)}, u32[]{:S(2)}) copy-start(bf16[256,1024]{1,0:T(8,128)(2,1)} %get-tuple-element.7) | copy-start | bytes 1572868
  49.0 1.2 %copy-start = (bf16[256,1024]{1,0:T(8,128)(2,1)S(1)}, bf16[256,1024]{1,0:T(8,128)(2,1)}, u32[]{:S(2)}) copy-start(bf16[256,1024]{1,0:T(8,128)(2,1)} %get-tuple-element.8) | copy-start | bytes 1572868
